TPU v7x, 256 devices: a whole 4x4x8 slice. The times are simulated.
256 devices in a mesh: blk: 128 (over z, x, y), rep: 2 (over core).
Axes of the slice: x: 4, y: 4, z: 8, core: 2. Of those that a mesh axis runs over, the one named last changes fastest.
Arguments:
- points: bfloat16 [4096, 1024], P('blk', 'rep'), may hold values from -16 to 16
- centroids: float32 [131072, 1024], P('blk', 'rep'), may hold values from -0.15 to 0.15
Outputs:
- new_centroids: float32 [131072, 1024], P('blk', 'rep')
- cluster_mass: float32 [131072], P('blk')
All inputs are finite; a program needn't handle non-finite values.
Results may differ from a plain program's by a relative error of at most 0.0065.
Values may be sent and summed in bfloat16 or wider, within the bound.
A program may use at most 128 MiB of HBM per device.

v0:
```python
import math

import jax
import jax.numpy as jnp
from jax import lax
from jax.sharding import PartitionSpec as P

ITERS = 3


SCALE = 3.0


def merged(array, axis, combine):
    everything = jax.tree.map(lambda part: lax.all_gather(part, axis), array)
    first = jax.tree.map(lambda part: part[0], everything)

    def turn(k, so_far):
        return combine(so_far, jax.tree.map(lambda part: part[k], everything))

    return lax.fori_loop(1, lax.axis_size(axis), turn, first)


def combine_pair(first, second):
    top_value = jnp.maximum(first[0], second[0])
    total = first[1] * jnp.exp(first[0] - top_value) + second[1] * jnp.exp(second[0] - top_value)
    return (top_value, total)


def block_totals(row_peak, row_mass):
    top_value = lax.pmax(row_peak, "blk")
    return (top_value, lax.psum(row_mass * jnp.exp(row_peak - top_value), "blk"))


def row_terms(logits, cluster_pot):
    moved = logits + cluster_pot[None, :]
    row_peak = jnp.max(moved, axis=1)
    return (row_peak, jnp.sum(jnp.exp(moved - row_peak[:, None]), axis=1))


def column_terms(logits, point_pot):
    shifted = logits + point_pot[:, None]
    col_peak = jnp.max(shifted, axis=0)
    return (col_peak, jnp.sum(jnp.exp(shifted - col_peak[None, :]), axis=0))


def per_device(points, centroids):
    blocks = lax.axis_size("blk")
    halves = lax.axis_size("rep")
    npts = points.shape[0] * blocks
    ncent = centroids.shape[0] * blocks
    log_points = math.log(npts)
    log_cents = math.log(ncent)
    prior = npts / ncent
    centroid_bf = centroids.astype(jnp.bfloat16)
    gathered = lax.all_gather(points, "blk", axis=0, tiled=True)
    own_rows = npts // halves
    logits = SCALE * lax.psum_scatter(
        jnp.dot(gathered, centroid_bf.T, preferred_element_type=jnp.float32),
        "rep",
        scatter_dimension=0,
        tiled=True,
    )
    point_pot = jnp.zeros((own_rows,), jnp.float32)
    for sweep in range(ITERS):
        col_peak, col_sum = column_terms(logits, point_pot)
        col_peak, col_sum = merged((col_peak, col_sum), "rep", combine_pair)
        cluster_pot = -log_cents - (col_peak + jnp.log(col_sum))
        row_peak, row_mass = row_terms(logits, cluster_pot)
        row_peak, row_mass = block_totals(row_peak, row_mass)
        point_pot = -log_points - (row_peak + jnp.log(row_mass))
    plan = jnp.exp(logits + point_pot[:, None] + cluster_pot[None, :] + log_points)
    mass = lax.psum(jnp.sum(plan, axis=0), "rep")
    weights = lax.all_gather(plan.astype(jnp.bfloat16), "rep", axis=0, tiled=True)
    numerator = jnp.dot(weights.T, gathered, preferred_element_type=jnp.float32)
    fresh = (numerator + prior * centroids) / (mass + prior)[:, None]
    return (fresh, mass)


def solution(mesh):
    return jax.shard_map(
        per_device,
        mesh=mesh,
        in_specs=(P("blk", "rep"), P("blk", "rep")),
        out_specs=(P("blk", "rep"), P("blk")),
        check_vma=False,
    )
```

profile of v0, /device:TPU:1, one launch (start us, length us, event | category | flops | bytes accessed | tf_op | source)
XLA Modules:
  0.0 2358.3 jit_solution(9816144250802139703)
XLA Ops:
  7.2 0.7 all-gather.9.cloned.1.call-update
  7.9 120.8 %all-gather.9.cloned.1.call-done = bf16[4096,512]{1,0:T(8,128)(2,1)} async-done(((bf16[32,512]{1,0:T(8,128)(2,1)}), bf16[4096,512]{1,0:T(8,128)(2,1)}) %all-gather.9.cloned.1.call-update) | async-done | bytes 4194320 | tf_op jit(solution)/shard_map/all_gather | solution.py:56
  128.7 13.1 fusion.3
  141.9 32.9 %reduce-scatter.2.cloned.1.call-done = f32[2048,1024]{1,0:T(8,128)} async-done(((f32[4096,1024]{1,0:T(8,128)}), f32[2048,1024]{1,0:T(8,128)}) %reduce-scatter.2.cloned.1.call-update) | async-done | bytes 8388624 | tf_op jit(solution)/shard_map/reduce_scatter | solution.py:58
  174.9 4.2 fusion.2
  179.1 1.9 all-gather
  181.0 1.4 exponential_reduce_fusion.5
  182.4 1.8 all-gather.1
  184.2 0.9 add_reduce_fusion.4
  185.2 298.7 %pmax.21 = f32[2048]{0:T(1024)S(1)} all-reduce(f32[2048]{0:T(1024)S(1)} %add_reduce_fusion.4), channel_id=1, replica_groups=mesh['blk'=128,'rep'=2] {'blk'}, use_global_device_ids=true, to_apply=%region_4.0 | all-reduce | flops 2048 | bytes 16384 | tf_op jit(solution)/shard_map/pmax | solution.py:31
  483.9 4.4 exponential_reduce_fusion.4
  488.3 291.6 %psum.28 = f32[2048]{0:T(1024)S(1)} all-reduce(f32[2048]{0:T(1024)S(1)} %exponential_multiply_fusion.2), channel_id=1, replica_groups=mesh['blk'=128,'rep'=2] {'blk'}, use_global_device_ids=true, to_apply=%region_6.0 | all-reduce | flops 2048 | bytes 16384 | tf_op jit(solution)/shard_map/psum | solution.py:32
  780.0 4.1 add_reduce_fusion.3
  784.0 111.6 %all-gather.2 = f32[2048]{0:T(1024)S(1)} all-gather(f32[1024]{0:T(1024)S(1)} %add_reduce_fusion.3), channel_id=4, replica_groups=mesh['blk'=128,'rep'=2] {'rep'}, dimensions={0}, use_global_device_ids=true | all-gather | bytes 12288 | tf_op jit(solution)/shard_map/all_gather | solution.py:15
  895.7 4.5 exponential_reduce_fusion.3
  900.2 1.8 all-gather.3
  902.1 0.9 add_reduce_fusion.2
  903.0 293.2 %pmax.22 = f32[2048]{0:T(1024)S(1)} all-reduce(f32[2048]{0:T(1024)S(1)} %add_reduce_fusion.2), channel_id=1, replica_groups=mesh['blk'=128,'rep'=2] {'blk'}, use_global_device_ids=true, to_apply=%region_10.0 | all-reduce | flops 2048 | bytes 16384 | tf_op jit(solution)/shard_map/pmax | solution.py:31
  1196.1 4.4 exponential_reduce_fusion.2
  1200.6 291.3 %psum.29 = f32[2048]{0:T(1024)S(1)} all-reduce(f32[2048]{0:T(1024)S(1)} %exponential_multiply_fusion.1), channel_id=1, replica_groups=mesh['blk'=128,'rep'=2] {'blk'}, use_global_device_ids=true, to_apply=%region_12.0 | all-reduce | flops 2048 | bytes 16384 | tf_op jit(solution)/shard_map/psum | solution.py:32
  1492.0 4.1 add_reduce_fusion.1
  1496.1 112.1 %all-gather.4 = f32[2048]{0:T(1024)S(1)} all-gather(f32[1024]{0:T(1024)S(1)} %add_reduce_fusion.1), channel_id=6, replica_groups=mesh['blk'=128,'rep'=2] {'rep'}, dimensions={0}, use_global_device_ids=true | all-gather | bytes 12288 | tf_op jit(solution)/shard_map/all_gather | solution.py:15
  1608.2 4.5 exponential_reduce_fusion.1
  1612.7 1.8 all-gather.5
  1614.5 0.9 add_reduce_fusion
  1615.4 293.0 %pmax.23 = f32[2048]{0:T(1024)S(1)} all-reduce(f32[2048]{0:T(1024)S(1)} %add_reduce_fusion), channel_id=1, replica_groups=mesh['blk'=128,'rep'=2] {'blk'}, use_global_device_ids=true, to_apply=%region_16.0 | all-reduce | flops 2048 | bytes 16384 | tf_op jit(solution)/shard_map/pmax | solution.py:31
  1908.4 4.5 exponential_reduce_fusion
  1912.9 291.3 %psum.30 = f32[2048]{0:T(1024)S(1)} all-reduce(f32[2048]{0:T(1024)S(1)} %exponential_multiply_fusion), channel_id=1, replica_groups=mesh['blk'=128,'rep'=2] {'blk'}, use_global_device_ids=true, to_apply=%region_18.0 | all-reduce | flops 2048 | bytes 16384 | tf_op jit(solution)/shard_map/psum | solution.py:32
  2204.3 6.0 fusion
  2210.3 112.9 %psum.31 = f32[1024]{0:T(1024)S(1)} all-reduce(f32[1024]{0:T(1024)S(1)} %get-tuple-element.38), channel_id=1, replica_groups=mesh['blk'=128,'rep'=2] {'rep'}, use_global_device_ids=true, to_apply=%region_20.0 | all-reduce | flops 1024 | bytes 8192 | tf_op jit(solution)/shard_map/psum | solution.py:73
  2323.1 18.2 all-gather.11.cloned.1.call-done
  2341.3 10.4 add_divide_fusion
  (37 shorter events, 0.3 us)
Async XLA Ops:
  7.2 121.6 %all-gather.9.cloned.1.call-start = ((), (), s32[]{:S(2)}) async-start(), calls=%async_computation.1 | async-start | bytes 4227072 | tf_op jit(solution)/shard_map/all_gather | solution.py:56
  7.9 167.0 %reduce-scatter.2.cloned.1.call-start = ((), (), s32[]{:S(2)}) async-start(), calls=%async_computation.2 | async-start | bytes 25165824 | tf_op jit(solution)/shard_map/reduce_scatter | solution.py:58
  141.9 2199.5 %all-gather.11.cloned.1.call-start = ((), (), s32[]{:S(2)}) async-start(), calls=%async_computation.3 | async-start | bytes 12582912 | tf_op jit(solution)/shard_map/all_gather | solution.py:74
  174.9 6.1 copy-start
  779.9 122.1 %slice-start = ((s8[8388608]{0:T(1024)(128)(4,1)}), s8[4194304]{0:T(1024)(128)(4,1)S(1)}, s32[]{:S(2)}) async-start(s8[8388608]{0:T(1024)(128)(4,1)} %bitcast.18), calls=%async_computation.4 | async-start | bytes 8388608
  895.7 6.3 slice-start.1
  1492.0 122.5 %slice-start.2 = ((s8[8388608]{0:T(1024)(128)(4,1)}), s8[4194304]{0:T(1024)(128)(4,1)S(1)}, s32[]{:S(2)}) async-start(s8[8388608]{0:T(1024)(128)(4,1)} %bitcast.20), calls=%async_computation.6 | async-start | bytes 8388608
  1608.2 6.3 slice-start.3
  2204.2 137.1 %copy-start.2 = (f32[1024,512]{1,0:T(8,128)S(1)}, f32[1024,512]{1,0:T(8,128)}, u32[]{:S(2)}) copy-start(f32[1024,512]{1,0:T(8,128)} %param.3) | copy-start | bytes 6291460
  2323.1 28.6 %copy-start.1 = (f32[1024]{0:T(1024)}, f32[1024]{0:T(1024)S(1)}, u32[]{:S(2)}) copy-start(f32[1024]{0:T(1024)S(1)} %psum.31) | copy-start | bytes 12292
Sparse Core Ops, SparseCore 0:
  11.6 117.0 all-gather.8
  142.0 32.8 reduce-scatter.1
  2210.4 130.9 all-gather.10
where the time goes:
time: 2360 us
  blocking collectives  2100 us (89%)
  waiting for transfers between devices  173 us (7%)
  other arithmetic  44.9 us (2%)
  matrix products  23.6 us (1%)
    pmax x3, blocking collectives, block_totals(): top_value = lax.pmax(row_peak, 'blk')  885 us
    psum x3, blocking collectives, block_totals(): lax.psum(row_mass * jnp.exp(row_peak - top_value), 'blk')  874 us
    all_gather x6, blocking collectives, merged(): everything = jax.tree.map(lambda part: lax.all_gather(part, axis), array)  231 us
    all_gather x1, waiting for transfers between devices, per_device(): gathered = lax.all_gather(points, 'blk', axis=0, tiled=True)  121 us
    psum x1, blocking collectives, per_device(): mass = lax.psum(jnp.sum(plan, axis=0), 'rep')  113 us
  transfers between devices with their start and end apart: 3, of which 3 were waited for; matrix products, arithmetic and copies ran while one was open for 0% of the time, Pallas kernels for 0%

commit v1 on v0

v1 whole, which is shorter than its diff:
```python
import math
from functools import reduce

import jax
import jax.numpy as jnp
from jax import lax
from jax.experimental import pallas as pl
from jax.experimental.pallas import tpu as pltpu
from jax.sharding import PartitionSpec as P

ITERS = 3
SCALE = 3.0
NZ, NX, NY = 8, 4, 4
CENTS = 1024
HALF = 512
ROWS = 16
PTS = NZ * NX * NY * ROWS
TILES = 8
LANES = 128
PBLOCKS = PTS // LANES
CGROUPS = CENTS // 8
LOG2_POINTS = 12.0
LOG2_CENTS = 17.0
PRIOR = 4096 / 131072
MESH = pl.DeviceIdType.MESH
GATHER_SEMS = 72
STAGE_SEMS = 14
STAGES = ((0, NY), (NY - 1, NX), (NY + NX - 2, NZ))


def kernel(points_ref, cent_ref, out_ref, mass_ref, pts, swap, cbf, logits, weights, col_max, col_sum,
           cpot, rpot, csend, crecv, rsend, rrecv, msend, mrecv, nsend, nrecv,
           gs, gr, its, itr, fs, fr):
    blk = lax.axis_index("blk")
    core = lax.axis_index("rep")
    other = 1 - core
    z = lax.div(blk, NX * NY)
    x = lax.rem(lax.div(blk, NY), NX)
    y = lax.rem(blk, NY)

    def on_z(i):
        return (lax.rem(i, NZ) * (NX * NY) + x * NY + y, core)

    def on_x(i):
        return (z * (NX * NY) + lax.rem(i, NX) * NY + y, core)

    def on_y(i):
        return (z * (NX * NY) + x * NY + lax.rem(i, NY), core)

    sibling = (blk, other)

    barrier = pltpu.get_barrier_semaphore()
    pl.semaphore_signal(barrier, inc=1, device_id=sibling, device_id_type=MESH)
    for pos, n, at in ((y, NY, on_y), (x, NX, on_x), (z, NZ, on_z)):
        for d in range(1, n):
            pl.semaphore_signal(barrier, inc=1, device_id=at(pos + d), device_id_type=MESH)
    pl.semaphore_wait(barrier, NZ + NX + NY - 2)

    pending = []
    count = [0]

    def remote(src, dst, send_sem, recv_sem, device):
        copy = pltpu.make_async_remote_copy(
            src_ref=src, dst_ref=dst, send_sem=send_sem, recv_sem=recv_sem,
            device_id=device, device_id_type=MESH)
        copy.start()
        return copy

    def place(ref, device):
        q = count[0]
        count[0] += 1
        copy = remote(ref, ref, gs.at[q], gr.at[q], device)
        pending.append(copy)
        return copy

    for j in range(4):
        lanes = slice(LANES * j, LANES * (j + 1))
        swap[j] = points_ref[pl.ds(pl.multiple_of(other * ROWS, ROWS), ROWS), lanes]
        pts[core * 4 + j, z, x, y] = points_ref[pl.ds(pl.multiple_of(core * ROWS, ROWS), ROWS), lanes]
    count[0] += 1
    swapped = remote(swap, pts.at[pl.ds(core * 4, 4), z, x, y], gs.at[0], gr.at[0], sibling)
    pending.append(swapped)
    cbf[core] = cent_ref[...].astype(jnp.bfloat16)
    cents_in = place(cbf.at[core], sibling)
    swapped.wait_recv()

    PZ, PX, PY = pl.ds(0, 2), pl.ds(2, 3), pl.ds(5, 3)
    first = []
    for d in (4, 3, 5, 2, 6, 1, 7):
        first.append(place(pts.at[PY, z, x, y], on_z(z + d)))
    for d in (2, 1, 3):
        first.append(place(pts.at[PX, z, x, y], on_y(y + d)))
        first.append(place(pts.at[PZ, z, x, y], on_x(x + d)))
    for copy in first:
        copy.wait_recv()

    def ring(n, pos, at, sub):
        right, left = at(pos + 1), at(pos + n - 1)
        prev_r, prev_l = {}, {}
        for s in range(1, n // 2 + 1):
            last = s == n // 2
            now_r, now_l = {}, {}
            for hr, hl in ((0, 1),) if last else ((0, 1), (1, 0)):
                if s > 1:
                    prev_r[hr].wait_recv()
                now_r[hr] = place(sub(lax.rem(pos + n - s + 1, n), hr), right)
                if s > 1:
                    prev_l[hl].wait_recv()
                now_l[hl] = place(sub(lax.rem(pos + s - 1, n), hl), left)
                yield
            if last:
                prev_r[1].wait_recv()
                prev_l[0].wait_recv()
            prev_r, prev_l = now_r, now_l
        prev_r[0].wait_recv()
        prev_l[1].wait_recv()
        yield

    def run(order, rings):
        for name in order:
            next(rings[name])

    run("zzxxyyzzxyzzzxyz", {
        "z": ring(NZ, z, on_z, lambda i, h: pts.at[PX, i, x, pl.ds(2 * h, 2)]),
        "x": ring(NX, x, on_x, lambda i, h: pts.at[PY, pl.ds(4 * h, 4), i, y]),
        "y": ring(NY, y, on_y, lambda i, h: pts.at[pl.ds(h, 1), z, :, i]),
    })
    run("xxyyzzzzxyzzzzxy", {
        "z": ring(NZ, z, on_z, lambda i, h: pts.at[pl.ds(h, 1), i]),
        "x": ring(NX, x, on_x, lambda i, h: pts.at[PX, pl.ds(4 * h, 4), i]),
        "y": ring(NY, y, on_y, lambda i, h: pts.at[PY, pl.ds(4 * h, 4), :, i]),
    })
    cents_in.wait_recv()

    def logit_block(b, carry):
        acc = None
        for h in range(2):
            block = jnp.concatenate(
                [pts[4 * h + j, b].reshape(NX * NY * ROWS, LANES) for j in range(4)], axis=1)
            part = lax.dot_general(cbf[h], block, (((1,), (1,)), ((), ())), preferred_element_type=jnp.float32)
            acc = part if acc is None else acc + part
        logits[:, pl.ds(pl.multiple_of(b * 256, 256), 256)] = acc * (SCALE * math.log2(math.e))
        return carry

    lax.fori_loop(0, NZ, logit_block, 0)

    lane = lax.broadcasted_iota(jnp.int32, (8, LANES), 1)

    def compact(b, acc, column):
        for q in range(16):
            acc = jnp.where(lane == 16 * b + q, jnp.broadcast_to(column[8 * q:8 * q + 8], (8, LANES)), acc)
        return acc

    def spread(dst, value):
        for g in range(CGROUPS):
            dst[8 * g:8 * g + 8, :] = jnp.broadcast_to(value[:, g:g + 1], (8, LANES))

    def merge(parts):
        top = reduce(jnp.maximum, parts)
        return top + jnp.log2(sum(jnp.exp2(p - top) for p in parts))

    rpot[...] = jnp.zeros((PBLOCKS, LANES), jnp.float32)

    def sweep(it, carry):
        def col_block(g, c):
            rows = pl.ds(pl.multiple_of(g * 16, 16), 16)
            vals = [logits[rows, LANES * j:LANES * (j + 1)] + rpot[j:j + 1, :] for j in range(PBLOCKS)]
            top = reduce(jnp.maximum, vals)
            col_max[rows, :] = top
            col_sum[rows, :] = sum(jnp.exp2(v - top) for v in vals)
            return c

        lax.fori_loop(0, CENTS // 16, col_block, 0)

        def col_finish(b, acc):
            rows = pl.ds(pl.multiple_of(b * 128, 128), 128)
            lane_max = col_max[rows, :]
            top = jnp.max(lane_max, axis=1, keepdims=True)
            total = jnp.sum(col_sum[rows, :] * jnp.exp2(lane_max - top), axis=1, keepdims=True)
            return compact(b, acc, top + jnp.log2(total))

        mine = lax.fori_loop(0, CENTS // 128, col_finish, jnp.zeros((8, LANES), jnp.float32))
        csend[it] = mine
        pair = remote(csend.at[it], crecv.at[it], its.at[it, STAGE_SEMS - 1], itr.at[it, STAGE_SEMS - 1], sibling)
        pair.wait_recv()
        spread(cpot, -LOG2_CENTS - merge([mine, crecv[it]]))

        for jb in range(4):
            def row_block(q, carry):
                tops, sums = carry
                rows = pl.ds(pl.multiple_of(q * 64, 64), 64)
                pot = cpot[rows, :].reshape(8, 8, LANES)
                new_tops, new_sums = [], []
                for j in range(4):
                    lanes = slice(512 * jb + LANES * j, 512 * jb + LANES * (j + 1))
                    vals = logits[rows, lanes].reshape(8, 8, LANES) + pot
                    top = jnp.maximum(tops[j], jnp.max(vals, axis=0))
                    new_sums.append(sums[j] * jnp.exp2(tops[j] - top) + jnp.sum(jnp.exp2(vals - top[None]), axis=0))
                    new_tops.append(top)
                return tuple(new_tops), tuple(new_sums)

            low = tuple(jnp.full((8, LANES), -3e38, jnp.float32) for _ in range(4))
            none = tuple(jnp.zeros((8, LANES), jnp.float32) for _ in range(4))
            tops, sums = lax.fori_loop(0, CENTS // 64, row_block, (low, none))
            for j in range(4):
                top = jnp.max(tops[j], axis=0, keepdims=True)
                total = jnp.sum(sums[j] * jnp.exp2(tops[j] - top), axis=0, keepdims=True)
                rsend[it, 0, 4 * jb + j:4 * jb + j + 1, :] = top + jnp.log2(total)

        merged = None
        sent = [pair]
        for k, (base, n) in enumerate(STAGES):
            pos, at = ((y, on_y), (x, on_x), (z, on_z))[k]
            if k:
                rsend[it, k] = merged
            copies = []
            for d in sorted(range(1, n), key=lambda d: -min(d, n - d)):
                q = base + d - 1
                copies.append(remote(rsend.at[it, k], rrecv.at[it, q], its.at[it, q], itr.at[it, q], at(pos + d)))
            for copy in copies:
                copy.wait_recv()
            merged = merge([rsend[it, k]] + [rrecv[it, base + d] for d in range(n - 1)])
            sent += copies
        rpot[...] = -LOG2_POINTS - merged
        for copy in sent:
            copy.wait_send()
        return carry

    lax.fori_loop(0, ITERS, sweep, 0)

    def plan_block(g, c):
        rows = pl.ds(pl.multiple_of(g * 16, 16), 16)
        pot = cpot[rows, :] + LOG2_POINTS
        total = None
        for j in range(PBLOCKS):
            lanes = slice(LANES * j, LANES * (j + 1))
            value = jnp.exp2(logits[rows, lanes] + rpot[j:j + 1, :] + pot)
            weights[rows, lanes] = value.astype(jnp.bfloat16)
            total = value if total is None else total + value
        col_sum[rows, :] = total
        return c

    lax.fori_loop(0, CENTS // 16, plan_block, 0)

    def mass_finish(b, acc):
        rows = pl.ds(pl.multiple_of(b * 128, 128), 128)
        return compact(b, acc, jnp.sum(col_sum[rows, :], axis=1, keepdims=True))

    mine = lax.fori_loop(0, CENTS // 128, mass_finish, jnp.zeros((8, LANES), jnp.float32))
    msend[...] = mine
    mass_in = remote(msend, mrecv, fs.at[2], fr.at[2], sibling)

    def product(tile):
        block = jnp.concatenate([pts[tile + j].reshape(PTS, LANES) for j in range(2)], axis=1)
        return jnp.dot(weights[...], block, preferred_element_type=jnp.float32)

    partial_in = []
    for b in range(2):
        nsend[b] = product(other * 4 + 2 * b)
        partial_in.append(remote(nsend.at[b], nrecv.at[b], fs.at[b], fr.at[b], sibling))

    mass_in.wait_recv()
    spread(col_sum, mine + mrecv[...])
    diagonal = (lax.broadcasted_iota(jnp.int32, (LANES, LANES), 0)
                == lax.broadcasted_iota(jnp.int32, (LANES, LANES), 1))
    for b in range(8):
        mass_ref[b:b + 1, :] = jnp.sum(
            jnp.where(diagonal, col_sum[LANES * b:LANES * (b + 1), :], 0.0), axis=0, keepdims=True)

    for b in range(2):
        lanes = slice(256 * b, 256 * (b + 1))
        own = product(core * 4 + 2 * b)
        partial_in[b].wait_recv()
        scale = 1.0 / (col_sum[...] + PRIOR)
        out_ref[:, lanes] = (own + nrecv[b] + PRIOR * cent_ref[:, lanes]) * jnp.concatenate([scale, scale], axis=1)

    for copy in pending + partial_in + [mass_in]:
        copy.wait_send()


def per_device(points, centroids):
    vmem = pl.BlockSpec(memory_space=pltpu.VMEM)
    f32, bf16 = jnp.float32, jnp.bfloat16
    fresh, mass = pl.pallas_call(
        kernel,
        out_shape=(jax.ShapeDtypeStruct((CENTS, HALF), f32), jax.ShapeDtypeStruct((8, LANES), f32)),
        in_specs=[vmem, vmem],
        out_specs=(vmem, vmem),
        scratch_shapes=[
            pltpu.VMEM((TILES, NZ, NX, NY, ROWS, LANES), bf16),
            pltpu.VMEM((4, ROWS, LANES), bf16),
            pltpu.VMEM((2, CENTS, HALF), bf16),
            pltpu.VMEM((CENTS, PTS), f32),
            pltpu.VMEM((CENTS, PTS), bf16),
            pltpu.VMEM((CENTS, LANES), f32),
            pltpu.VMEM((CENTS, LANES), f32),
            pltpu.VMEM((CENTS, LANES), f32),
            pltpu.VMEM((PBLOCKS, LANES), f32),
            pltpu.VMEM((ITERS, 8, LANES), f32),
            pltpu.VMEM((ITERS, 8, LANES), f32),
            pltpu.VMEM((ITERS, 3, PBLOCKS, LANES), f32),
            pltpu.VMEM((ITERS, STAGE_SEMS - 1, PBLOCKS, LANES), f32),
            pltpu.VMEM((8, LANES), f32),
            pltpu.VMEM((8, LANES), f32),
            pltpu.VMEM((2, CENTS, 256), f32),
            pltpu.VMEM((2, CENTS, 256), f32),
            pltpu.SemaphoreType.DMA((GATHER_SEMS,)),
            pltpu.SemaphoreType.DMA((GATHER_SEMS,)),
            pltpu.SemaphoreType.DMA((ITERS, STAGE_SEMS)),
            pltpu.SemaphoreType.DMA((ITERS, STAGE_SEMS)),
            pltpu.SemaphoreType.DMA((3,)),
            pltpu.SemaphoreType.DMA((3,)),
        ],
        compiler_params=pltpu.CompilerParams(
            collective_id=0, has_side_effects=True, vmem_limit_bytes=60 * 1024 * 1024),
    )(points, centroids)
    return fresh, mass.reshape(CENTS)


def solution(mesh):
    return jax.shard_map(
        per_device,
        mesh=mesh,
        in_specs=(P("blk", "rep"), P("blk", "rep")),
        out_specs=(P("blk", "rep"), P("blk")),
        check_vma=False,
    )
```

time: 2360 us -> 130 us (0.06)
  blocking collectives: 2100 us -> 0 us
  waiting for transfers between devices: 173 us -> 0 us
  Pallas kernels: 0 us -> 126 us
  other arithmetic: 44.9 us -> 0 us
  matrix products: 23.6 us -> 0 us
    psum x4 -> x0, blocking collectives: 987 us -> none  [the longest x3 874 us: block_totals(): lax.psum(row_mass * jnp.exp(row_peak - top_value), 'blk')]
    pmax x3 -> x0, blocking collectives: 885 us -> none  [block_totals(): top_value = lax.pmax(row_peak, 'blk')]
    all_gather x6 -> x0, blocking collectives: 231 us -> none  [merged(): everything = jax.tree.map(lambda part: lax.all_gather(part, axis), array)]
    all_gather x2 -> x0, waiting for transfers between devices: 139 us -> none  [the longest x1 121 us: per_device(): gathered = lax.all_gather(points, 'blk', axis=0, tiled=True)]
    pallas_call x0 -> x1, Pallas kernels: none -> 126 us  [per_device(): pl.pallas_call(kernel, out_shape=(jax.ShapeDtypeStruct((CENTS, HALF), f32...]
    reduce_scatter x1 -> x0, waiting for transfers between devices: 32.9 us -> none  [per_device(): lax.psum_scatter(jnp.dot(gathered, centroid_bf.T, preferred_element_type=...]
    reduce_sum x7 -> x0, other arithmetic: 29.8 us -> none  [the longest x3 13.3 us: row_terms(): return (row_peak, jnp.sum(jnp.exp(moved - row_peak[:, None]), axis=1))]
  transfers between devices with their start and end apart: 3 -> 0, of which waited for: 3 -> 0; matrix products, arithmetic and copies ran while one was open for 0% -> 0% of each run, Pallas kernels for 0% -> 0%
where the time goes in v1:
time: 130 us
  Pallas kernels  126 us (97%)
  local copies, waits for them, and re-layouts  3.68 us (3%)
    pallas_call x1, Pallas kernels, per_device(): pl.pallas_call(kernel, out_shape=(jax.ShapeDtypeStruct((CENTS, HALF), f32...  126 us
    unnamed x4, local copies, waits for them, and re-layouts  3.68 us

profile of v1, /device:TPU:1, one launch (start us, length us, event | category | flops | bytes accessed | tf_op | source)
XLA Modules:
  0.0 130.1 jit_solution(10800478292947940065)
XLA Ops:
  0.6 125.8 %shard_map.41 = (f32[1024,512]{1,0:T(8,128)}, f32[8,128]{1,0:T(8,128)}) custom-call(bf16[32,512]{1,0:T(8,128)(2,1)} %points_ref.1, f32[1024,512]{1,0:T(8,128)} %cent_ref.1), custom_call_target="tpu_custom_call" | custom-call | tf_op jit(solution)/shard_map/pallas_call | solution.py:284
  126.5 0.0 copy-start
  126.5 3.1 %copy.6 = f32[1024,512]{1,0:T(8,128)} copy(f32[1024,512]{1,0:T(8,128)} %get-tuple-element.8) | data formatting | bytes 4194304
  129.5 0.0 copy-done
  129.6 0.6 copy.7
Async XLA Ops:
  126.5 3.1 %copy-start = (f32[8,128]{1,0:T(8,128)S(1)}, f32[8,128]{1,0:T(8,128)}, u32[]{:S(2)}) copy-start(f32[8,128]{1,0:T(8,128)} %get-tuple-element.5) | copy-start | bytes 12292

commit v2 on v1

v2 whole, which is shorter than its diff:
```python
import math
from functools import reduce

import jax
import jax.numpy as jnp
from jax import lax
from jax.experimental import pallas as pl
from jax.experimental.pallas import tpu as pltpu
from jax.sharding import PartitionSpec as P

ITERS = 3
SCALE = 3.0
NZ, NX, NY = 8, 4, 4
CENTS = 1024
HALF = 512
ROWS = 16
PTS = NZ * NX * NY * ROWS
TILES = 8
LANES = 128
PBLOCKS = PTS // LANES
CGROUPS = CENTS // 8
LOG2_POINTS = 12.0
LOG2_CENTS = 17.0
PRIOR = 4096 / 131072
MESH = pl.DeviceIdType.MESH
GATHER_SEMS = 134
PLANE = tuple((dx, dy) for dx in range(NX) for dy in range(NY) if dx or dy)
STAGES = ((0, len(PLANE)), (len(PLANE), NZ - 1))
STAGE_SEMS = len(PLANE) + NZ


def kernel(points_hbm, cent_hbm, out_ref, mass_ref, points_ref, cent_ref, pts, swap, cbf, logits, weights,
           col_max, col_sum, cpot, rpot, csend, crecv, rsend, rrecv, msend, mrecv, nsend, nrecv,
           gs, gr, its, itr, fs, fr, ls):
    blk = lax.axis_index("blk")
    core = lax.axis_index("rep")
    other = 1 - core
    z = lax.div(blk, NX * NY)
    x = lax.rem(lax.div(blk, NY), NX)
    y = lax.rem(blk, NY)

    def at(dz, dx, dy):
        return (lax.rem(z + dz, NZ) * (NX * NY) + lax.rem(x + dx, NX) * NY + lax.rem(y + dy, NY), core)

    sibling = (blk, other)

    points_in = pltpu.make_async_copy(points_hbm, points_ref, ls.at[0])
    points_in.start()
    own_in = pltpu.make_async_copy(cent_hbm, cent_ref, ls.at[1])
    own_in.start()
    barrier = pltpu.get_barrier_semaphore()
    pl.semaphore_signal(barrier, inc=1, device_id=sibling, device_id_type=MESH)
    for dx, dy in PLANE:
        pl.semaphore_signal(barrier, inc=1, device_id=at(0, dx, dy), device_id_type=MESH)
    for d in range(1, NZ):
        pl.semaphore_signal(barrier, inc=1, device_id=at(d, 0, 0), device_id_type=MESH)
    points_in.wait()
    for j in range(4):
        lanes = slice(LANES * j, LANES * (j + 1))
        swap[j] = points_ref[pl.ds(pl.multiple_of(other * ROWS, ROWS), ROWS), lanes]
        pts[core * 4 + j, z, x, y] = points_ref[pl.ds(pl.multiple_of(core * ROWS, ROWS), ROWS), lanes]
    pl.semaphore_wait(barrier, STAGE_SEMS)

    pending = []
    count = [0]

    def remote(src, dst, send_sem, recv_sem, device):
        copy = pltpu.make_async_remote_copy(
            src_ref=src, dst_ref=dst, send_sem=send_sem, recv_sem=recv_sem,
            device_id=device, device_id_type=MESH)
        copy.start()
        return copy

    def place(ref, device):
        q = count[0]
        count[0] += 1
        copy = remote(ref, ref, gs.at[q], gr.at[q], device)
        pending.append(copy)
        return copy

    count[0] += 1
    swapped = remote(swap, pts.at[pl.ds(core * 4, 4), z, x, y], gs.at[0], gr.at[0], sibling)
    pending.append(swapped)
    own_in.wait()
    cbf[core] = cent_ref[...].astype(jnp.bfloat16)
    cents_in = place(cbf.at[core], sibling)
    swapped.wait_recv()

    PZ, PX, PY, PXY = pl.ds(0, 2), pl.ds(2, 3), pl.ds(5, 3), pl.ds(2, 6)
    along_z = {}
    for d in (4, 3, 5, 2, 6, 1, 7):
        along_z[NZ - d] = place(pts.at[PXY, z, x, y], at(d, 0, 0))
    second, third, fourth, tasks = {}, {}, {}, []

    def spread_layer(dz):
        if dz:
            along_z[dz].wait_recv()
        layer = lax.rem(z + dz, NZ)
        second[dz] = []
        for d in (2, 1, 3):
            second[dz].append(place(pts.at[PX, layer, x, y], at(0, 0, d)))
            second[dz].append(place(pts.at[PY, layer, x, y], at(0, d, 0)))

    def x_line(dz, dx):
        return pts.at[PX, lax.rem(z + dz, NZ), lax.rem(x + dx, NX)]

    def y_line(dz, dy):
        return pts.at[PY, lax.rem(z + dz, NZ), :, lax.rem(y + dy, NY)]

    def send_lines(dz):
        for copy in second[dz]:
            copy.wait_recv()
        third[dz] = {}
        for d in (1, 3):
            third[dz]["x", d] = place(x_line(dz, 0), at(0, d, 0))
            third[dz]["y", d] = place(y_line(dz, 0), at(0, 0, d))

    def forward_lines(dz):
        d = 1 if dz % 2 else 3
        third[dz]["x", d].wait_recv()
        right = place(x_line(dz, NX - d), at(0, d, 0))
        third[dz]["y", d].wait_recv()
        fourth[dz] = (right, place(y_line(dz, NY - d), at(0, 0, d)))

    def layer_done(dz):
        d = 3 if dz % 2 else 1
        third[dz]["x", d].wait_recv()
        third[dz]["y", d].wait_recv()
        for copy in fourth[dz]:
            copy.wait_recv()

    def z_ring():
        def block(d, h):
            return pts.at[pl.ds(h, 1), lax.rem(z + d, NZ)]

        up, down = at(1, 0, 0), at(NZ - 1, 0, 0)
        prev_u, prev_d = {}, {}
        for s in range(1, NZ // 2 + 1):
            last = s == NZ // 2
            now_u, now_d = {}, {}
            for hu, hd in ((0, 1),) if last else ((0, 1), (1, 0)):
                if s > 1:
                    prev_u[hu].wait_recv()
                now_u[hu] = place(block(NZ - s + 1, hu), up)
                if s > 1:
                    prev_d[hd].wait_recv()
                now_d[hd] = place(block(s - 1, hd), down)
            if last:
                prev_u[1].wait_recv()
                prev_d[0].wait_recv()
            prev_u, prev_d = now_u, now_d
            yield
        prev_u[0].wait_recv()
        prev_d[1].wait_recv()
        yield

    ring = z_ring()
    spread_layer(0)
    plane = [place(pts.at[PZ, z, x, y], at(0, dx, dy)) for dx, dy in PLANE]

    def plane_done():
        for copy in plane:
            copy.wait_recv()
        next(ring)

    def logit_block(dz):
        layer = lax.rem(z + dz, NZ)
        acc = None
        for h in range(2):
            block = jnp.concatenate(
                [pts[4 * h + j, layer].reshape(NX * NY * ROWS, LANES) for j in range(4)], axis=1)
            part = lax.dot_general(cbf[h], block, (((1,), (1,)), ((), ())), preferred_element_type=jnp.float32)
            acc = part if acc is None else acc + part
        logits[:, pl.ds(pl.multiple_of(layer * 256, 256), 256)] = acc * (SCALE * math.log2(math.e))

    near, far = {0: 0, 1: 1, 7: 1, 2: 2, 6: 2, 3: 3, 5: 3, 4: 4}, (0, 1, 7, 2, 6, 3, 5, 4)
    for dz in far:
        r = near[dz]
        if dz:
            tasks.append(((0, 3.5, 4.3, 5.2, 6.0)[r], spread_layer, (dz,)))
        tasks.append(((3.9, 7.3, 8.2, 9.2, 10.2)[r], send_lines, (dz,)))
        tasks.append(((7.4, 10.9, 11.8, 13.0, 14.0)[r], forward_lines, (dz,)))
        tasks.append(((10.95, 14.8, 15.5, 16.5, 18.2)[r], layer_done, (dz,)))
        tasks.append(((10.95, 14.8, 15.5, 16.5, 18.2)[r], logit_block, (dz,)))
    tasks.append((5.1, plane_done, ()))
    for t in (8.3, 11.5, 14.6, 18.1):
        tasks.append((t, next, (ring,)))
    tasks.append((10.9, cents_in.wait_recv, ()))
    for _, task, args in sorted(tasks, key=lambda t: t[0]):
        task(*args)

    lane = lax.broadcasted_iota(jnp.int32, (8, LANES), 1)

    def compact(column):
        acc = jnp.zeros((8, LANES), jnp.float32)
        for g in range(CGROUPS):
            acc = jnp.where(lane == g, jnp.broadcast_to(column[8 * g:8 * g + 8], (8, LANES)), acc)
        return acc

    def spread(dst, value):
        for g in range(CGROUPS):
            dst[8 * g:8 * g + 8, :] = jnp.broadcast_to(value[:, g:g + 1], (8, LANES))

    def merge(parts):
        top = reduce(jnp.maximum, parts)
        return top + jnp.log2(sum(jnp.exp2(p - top) for p in parts))

    rpot[...] = jnp.zeros((PBLOCKS, LANES), jnp.float32)

    def sweep(it, carry):
        def col_block(g, c):
            rows = pl.ds(pl.multiple_of(g * 16, 16), 16)
            vals = [logits[rows, LANES * j:LANES * (j + 1)] + rpot[j:j + 1, :] for j in range(PBLOCKS)]
            top = reduce(jnp.maximum, vals)
            col_max[rows, :] = top
            col_sum[rows, :] = sum(jnp.exp2(v - top) for v in vals)
            return c

        lax.fori_loop(0, CENTS // 16, col_block, 0, unroll=4)

        top = jnp.max(col_max[...], axis=1, keepdims=True)
        total = jnp.sum(col_sum[...] * jnp.exp2(col_max[...] - top), axis=1, keepdims=True)
        mine = compact(top + jnp.log2(total))
        csend[it] = mine
        pair = remote(csend.at[it], crecv.at[it], its.at[it, STAGE_SEMS - 1], itr.at[it, STAGE_SEMS - 1], sibling)
        pair.wait_recv()
        spread(cpot, -LOG2_CENTS - merge([mine, crecv[it]]))

        for jb in range(4):
            def row_block(q, carry):
                tops, sums = carry
                rows = pl.ds(pl.multiple_of(q * 64, 64), 64)
                pot = cpot[rows, :].reshape(8, 8, LANES)
                new_tops, new_sums = [], []
                for j in range(4):
                    lanes = slice(512 * jb + LANES * j, 512 * jb + LANES * (j + 1))
                    vals = logits[rows, lanes].reshape(8, 8, LANES) + pot
                    top = jnp.maximum(tops[j], jnp.max(vals, axis=0))
                    new_sums.append(sums[j] * jnp.exp2(tops[j] - top) + jnp.sum(jnp.exp2(vals - top[None]), axis=0))
                    new_tops.append(top)
                return tuple(new_tops), tuple(new_sums)

            low = tuple(jnp.full((8, LANES), -3e38, jnp.float32) for _ in range(4))
            none = tuple(jnp.zeros((8, LANES), jnp.float32) for _ in range(4))
            tops, sums = lax.fori_loop(0, CENTS // 64, row_block, (low, none), unroll=4)
            for j in range(4):
                top = jnp.max(tops[j], axis=0, keepdims=True)
                total = jnp.sum(sums[j] * jnp.exp2(tops[j] - top), axis=0, keepdims=True)
                rsend[it, 0, 4 * jb + j:4 * jb + j + 1, :] = top + jnp.log2(total)

        merged = None
        sent = [pair]
        for k, (base, n) in enumerate(STAGES):
            peers = [at(0, dx, dy) for dx, dy in PLANE] if k == 0 else [at(d, 0, 0) for d in range(1, NZ)]
            if k:
                rsend[it, k] = merged
            copies = [remote(rsend.at[it, k], rrecv.at[it, base + q], its.at[it, base + q], itr.at[it, base + q], peer)
                      for q, peer in enumerate(peers)]
            for copy in copies:
                copy.wait_recv()
            merged = merge([rsend[it, k]] + [rrecv[it, base + q] for q in range(n)])
            sent += copies
        rpot[...] = -LOG2_POINTS - merged
        for copy in sent:
            copy.wait_send()
        return carry

    lax.fori_loop(0, ITERS, sweep, 0)

    def plan_block(g, c):
        rows = pl.ds(pl.multiple_of(g * 16, 16), 16)
        pot = cpot[rows, :] + LOG2_POINTS
        total = None
        for j in range(PBLOCKS):
            lanes = slice(LANES * j, LANES * (j + 1))
            value = jnp.exp2(logits[rows, lanes] + rpot[j:j + 1, :] + pot)
            weights[rows, lanes] = value.astype(jnp.bfloat16)
            total = value if total is None else total + value
        col_sum[rows, :] = total
        return c

    lax.fori_loop(0, CENTS // 16, plan_block, 0, unroll=4)

    mine = compact(jnp.sum(col_sum[...], axis=1, keepdims=True))
    msend[...] = mine
    mass_in = remote(msend, mrecv, fs.at[2], fr.at[2], sibling)

    def product(tile):
        block = jnp.concatenate([pts[tile + j].reshape(PTS, LANES) for j in range(2)], axis=1)
        return jnp.dot(weights[...], block, preferred_element_type=jnp.float32)

    partial_in = []
    for b in range(2):
        nsend[b] = product(other * 4 + 2 * b)
        partial_in.append(remote(nsend.at[b], nrecv.at[b], fs.at[b], fr.at[b], sibling))

    mass_in.wait_recv()
    spread(col_sum, mine + mrecv[...])
    diagonal = (lax.broadcasted_iota(jnp.int32, (LANES, LANES), 0)
                == lax.broadcasted_iota(jnp.int32, (LANES, LANES), 1))
    for b in range(8):
        mass_ref[b:b + 1, :] = jnp.sum(
            jnp.where(diagonal, col_sum[LANES * b:LANES * (b + 1), :], 0.0), axis=0, keepdims=True)

    for b in range(2):
        lanes = slice(256 * b, 256 * (b + 1))
        own = product(core * 4 + 2 * b)
        partial_in[b].wait_recv()
        scale = 1.0 / (col_sum[...] + PRIOR)
        out_ref[:, lanes] = (own + nrecv[b] + PRIOR * cent_ref[:, lanes]) * jnp.concatenate([scale, scale], axis=1)

    for copy in pending + partial_in + [mass_in]:
        copy.wait_send()


def per_device(points, centroids):
    vmem = pl.BlockSpec(memory_space=pltpu.VMEM)
    hbm = pl.BlockSpec(memory_space=pl.ANY)
    f32, bf16 = jnp.float32, jnp.bfloat16
    fresh, mass = pl.pallas_call(
        kernel,
        out_shape=(jax.ShapeDtypeStruct((CENTS, HALF), f32), jax.ShapeDtypeStruct((8, LANES), f32)),
        in_specs=[hbm, hbm],
        out_specs=(vmem, vmem),
        scratch_shapes=[
            pltpu.VMEM((2 * ROWS, HALF), bf16),
            pltpu.VMEM((CENTS, HALF), f32),
            pltpu.VMEM((TILES, NZ, NX, NY, ROWS, LANES), bf16),
            pltpu.VMEM((4, ROWS, LANES), bf16),
            pltpu.VMEM((2, CENTS, HALF), bf16),
            pltpu.VMEM((CENTS, PTS), f32),
            pltpu.VMEM((CENTS, PTS), bf16),
            pltpu.VMEM((CENTS, LANES), f32),
            pltpu.VMEM((CENTS, LANES), f32),
            pltpu.VMEM((CENTS, LANES), f32),
            pltpu.VMEM((PBLOCKS, LANES), f32),
            pltpu.VMEM((ITERS, 8, LANES), f32),
            pltpu.VMEM((ITERS, 8, LANES), f32),
            pltpu.VMEM((ITERS, len(STAGES), PBLOCKS, LANES), f32),
            pltpu.VMEM((ITERS, STAGE_SEMS - 1, PBLOCKS, LANES), f32),
            pltpu.VMEM((8, LANES), f32),
            pltpu.VMEM((8, LANES), f32),
            pltpu.VMEM((2, CENTS, 256), f32),
            pltpu.VMEM((2, CENTS, 256), f32),
            pltpu.SemaphoreType.DMA((GATHER_SEMS,)),
            pltpu.SemaphoreType.DMA((GATHER_SEMS,)),
            pltpu.SemaphoreType.DMA((ITERS, STAGE_SEMS)),
            pltpu.SemaphoreType.DMA((ITERS, STAGE_SEMS)),
            pltpu.SemaphoreType.DMA((3,)),
            pltpu.SemaphoreType.DMA((3,)),
            pltpu.SemaphoreType.DMA((2,)),
        ],
        compiler_params=pltpu.CompilerParams(
            collective_id=0, has_side_effects=True, vmem_limit_bytes=60 * 1024 * 1024),
    )(points, centroids)
    return fresh, mass.reshape(CENTS)


def solution(mesh):
    return jax.shard_map(
        per_device,
        mesh=mesh,
        in_specs=(P("blk", "rep"), P("blk", "rep")),
        out_specs=(P("blk", "rep"), P("blk")),
        check_vma=False,
    )
```

time: 130 us -> 110 us (0.85)
  Pallas kernels: 126 us -> 105 us
    pallas_call x1, Pallas kernels: 126 us -> 105 us  [per_device(): pl.pallas_call(kernel, out_shape=(jax.ShapeDtypeStruct((CENTS, HALF), f32...]
where the time goes in v2:
time: 110 us
  Pallas kernels  105 us (95%)
  local copies, waits for them, and re-layouts  3.68 us (3%)
    pallas_call x1, Pallas kernels, per_device(): pl.pallas_call(kernel, out_shape=(jax.ShapeDtypeStruct((CENTS, HALF), f32...  105 us
    unnamed x4, local copies, waits for them, and re-layouts  3.68 us

profile of v2, /device:TPU:1, one launch (start us, length us, event | category | flops | bytes accessed | tf_op | source)
XLA Modules:
  0.0 109.7 jit_solution(14430835261694058861)
XLA Ops:
  0.6 105.4 %shard_map.41 = (f32[1024,512]{1,0:T(8,128)}, f32[8,128]{1,0:T(8,128)}) custom-call(bf16[32,512]{1,0:T(8,128)(2,1)} %points_hbm.1, f32[1024,512]{1,0:T(8,128)} %cent_hbm.1), custom_call_target="tpu_custom_call" | custom-call | tf_op jit(solution)/shard_map/pallas_call | solution.py:320
  106.0 0.0 copy-start
  106.0 3.1 %copy.6 = f32[1024,512]{1,0:T(8,128)} copy(f32[1024,512]{1,0:T(8,128)} %get-tuple-element.8) | data formatting | bytes 4194304
  109.1 0.0 copy-done
  109.1 0.6 copy.7
Async XLA Ops:
  106.0 3.1 %copy-start = (f32[8,128]{1,0:T(8,128)S(1)}, f32[8,128]{1,0:T(8,128)}, u32[]{:S(2)}) copy-start(f32[8,128]{1,0:T(8,128)} %get-tuple-element.5) | copy-start | bytes 12292

commit v3 on v2

--- a/solution.py
+++ b/solution.py
@@ -22,15 +22,16 @@
 LOG2_POINTS = 12.0
 LOG2_CENTS = 17.0
 PRIOR = 4096 / 131072
+CHUNK = 256
 MESH = pl.DeviceIdType.MESH
-GATHER_SEMS = 134
+GATHER_SEMS = 148
 PLANE = tuple((dx, dy) for dx in range(NX) for dy in range(NY) if dx or dy)
 STAGES = ((0, len(PLANE)), (len(PLANE), NZ - 1))
 STAGE_SEMS = len(PLANE) + NZ
 
 
 def kernel(points_hbm, cent_hbm, out_ref, mass_ref, points_ref, cent_ref, pts, swap, cbf, logits, weights,
-           col_max, col_sum, cpot, rpot, csend, crecv, rsend, rrecv, msend, mrecv, nsend, nrecv,
+           col_max, col_sum, cpot, rpot, csend, crecv, rsend, rrecv, msend, mrecv, nsend, nrecv, own, fresh,
            gs, gr, its, itr, fs, fr, ls):
     blk = lax.axis_index("blk")
     core = lax.axis_index("rep")
@@ -88,9 +89,7 @@
 
     PZ, PX, PY, PXY = pl.ds(0, 2), pl.ds(2, 3), pl.ds(5, 3), pl.ds(2, 6)
     along_z = {}
-    for d in (4, 3, 5, 2, 6, 1, 7):
-        along_z[NZ - d] = place(pts.at[PXY, z, x, y], at(d, 0, 0))
-    second, third, fourth, tasks = {}, {}, {}, []
+    second, third, fourth = {}, {}, {}
 
     def spread_layer(dz):
         if dz:
@@ -129,65 +128,62 @@
         for copy in fourth[dz]:
             copy.wait_recv()
 
-    def z_ring():
-        def block(d, h):
-            return pts.at[pl.ds(h, 1), lax.rem(z + d, NZ)]
-
-        up, down = at(1, 0, 0), at(NZ - 1, 0, 0)
-        prev_u, prev_d = {}, {}
-        for s in range(1, NZ // 2 + 1):
-            last = s == NZ // 2
-            now_u, now_d = {}, {}
-            for hu, hd in ((0, 1),) if last else ((0, 1), (1, 0)):
-                if s > 1:
-                    prev_u[hu].wait_recv()
-                now_u[hu] = place(block(NZ - s + 1, hu), up)
-                if s > 1:
-                    prev_d[hd].wait_recv()
-                now_d[hd] = place(block(s - 1, hd), down)
-            if last:
-                prev_u[1].wait_recv()
-                prev_d[0].wait_recv()
-            prev_u, prev_d = now_u, now_d
-            yield
-        prev_u[0].wait_recv()
-        prev_d[1].wait_recv()
-        yield
-
-    ring = z_ring()
+    def z_block(d, c):
+        return pts.at[PZ, lax.rem(z + d, NZ), lax.rem(x + c, NX)]
+
+    plane, up, down = {}, {}, {}
+
+    def z_step(s, c):
+        if s > 1:
+            up[s - 1, c].wait_recv()
+            down[s - 1, c].wait_recv()
+        else:
+            for copy in plane[c]:
+                copy.wait_recv()
+        if s < NZ // 2 or c < 2:
+            up[s, c] = place(z_block(NZ - s + 1, c), at(1, 0, 0))
+        if s < NZ // 2 or c >= 2:
+            down[s, c] = place(z_block(s - 1, c), at(NZ - 1, 0, 0))
+
+    for d in (1, 7, 2, 6, 3, 5, 4):
+        along_z[NZ - d] = place(pts.at[PXY, z, x, y], at(d, 0, 0))
     spread_layer(0)
-    plane = [place(pts.at[PZ, z, x, y], at(0, dx, dy)) for dx, dy in PLANE]
-
-    def plane_done():
-        for copy in plane:
-            copy.wait_recv()
-        next(ring)
+    for dx in (0, 2, 1, 3):
+        plane[(NX - dx) % NX] = [place(pts.at[PZ, z, x, y], at(0, dx, dy)) for dy in range(NY) if dx or dy]
 
     def logit_block(dz):
+        layer_done(dz)
+        if dz == 0:
+            cents_in.wait_recv()
+        elif dz == NZ // 2:
+            for copy in (up[dz, 0], up[dz, 1], down[dz, 2], down[dz, 3]):
+                copy.wait_recv()
         layer = lax.rem(z + dz, NZ)
-        acc = None
-        for h in range(2):
-            block = jnp.concatenate(
-                [pts[4 * h + j, layer].reshape(NX * NY * ROWS, LANES) for j in range(4)], axis=1)
-            part = lax.dot_general(cbf[h], block, (((1,), (1,)), ((), ())), preferred_element_type=jnp.float32)
-            acc = part if acc is None else acc + part
-        logits[:, pl.ds(pl.multiple_of(layer * 256, 256), 256)] = acc * (SCALE * math.log2(math.e))
-
-    near, far = {0: 0, 1: 1, 7: 1, 2: 2, 6: 2, 3: 3, 5: 3, 4: 4}, (0, 1, 7, 2, 6, 3, 5, 4)
-    for dz in far:
-        r = near[dz]
-        if dz:
-            tasks.append(((0, 3.5, 4.3, 5.2, 6.0)[r], spread_layer, (dz,)))
-        tasks.append(((3.9, 7.3, 8.2, 9.2, 10.2)[r], send_lines, (dz,)))
-        tasks.append(((7.4, 10.9, 11.8, 13.0, 14.0)[r], forward_lines, (dz,)))
-        tasks.append(((10.95, 14.8, 15.5, 16.5, 18.2)[r], layer_done, (dz,)))
-        tasks.append(((10.95, 14.8, 15.5, 16.5, 18.2)[r], logit_block, (dz,)))
-    tasks.append((5.1, plane_done, ()))
-    for t in (8.3, 11.5, 14.6, 18.1):
-        tasks.append((t, next, (ring,)))
-    tasks.append((10.9, cents_in.wait_recv, ()))
-    for _, task, args in sorted(tasks, key=lambda t: t[0]):
-        task(*args)
+        lanes = pl.ds(pl.multiple_of(layer * 256, 256), 256)
+
+        def part(m, carry):
+            rows = pl.ds(pl.multiple_of(m * CHUNK, CHUNK), CHUNK)
+            acc = None
+            for h in range(2):
+                block = jnp.concatenate(
+                    [pts[4 * h + j, layer].reshape(NX * NY * ROWS, LANES) for j in range(4)], axis=1)
+                term = lax.dot_general(
+                    cbf[h, rows, :], block, (((1,), (1,)), ((), ())), preferred_element_type=jnp.float32)
+                acc = term if acc is None else acc + term
+            logits[rows, lanes] = acc * (SCALE * math.log2(math.e))
+            return carry
+
+        lax.fori_loop(0, CENTS // CHUNK, part, 0)
+
+    tasks = {"a": spread_layer, "b": send_lines, "c": forward_lines, "r": z_step, "m": logit_block}
+    for step in (
+        ("a", 1), ("a", 7), ("b", 0), ("r", 1, 0), ("r", 1, 1), ("r", 1, 3), ("r", 1, 2), ("a", 2), ("a", 6), ("b", 1),
+        ("b", 7), ("a", 3), ("a", 5), ("c", 0), ("r", 2, 0), ("r", 2, 1), ("r", 2, 3), ("r", 2, 2), ("a", 4), ("b", 2),
+        ("b", 6), ("c", 1), ("c", 7), ("m", 0), ("b", 3), ("b", 5), ("r", 3, 0), ("r", 3, 1), ("r", 3, 3), ("r", 3, 2),
+        ("c", 2), ("c", 6), ("m", 1), ("m", 7), ("b", 4), ("r", 4, 0), ("r", 4, 1), ("r", 4, 3), ("r", 4, 2), ("c", 3),
+        ("c", 5), ("m", 2), ("m", 6), ("c", 4), ("m", 3), ("m", 5), ("m", 4),
+    ):
+        tasks[step[0]](*step[1:])
 
     lane = lax.broadcasted_iota(jnp.int32, (8, LANES), 1)
 
@@ -285,13 +281,19 @@
     msend[...] = mine
     mass_in = remote(msend, mrecv, fs.at[2], fr.at[2], sibling)
 
-    def product(tile):
+    def product(tile, dst):
         block = jnp.concatenate([pts[tile + j].reshape(PTS, LANES) for j in range(2)], axis=1)
-        return jnp.dot(weights[...], block, preferred_element_type=jnp.float32)
+
+        def part(m, carry):
+            rows = pl.ds(pl.multiple_of(m * CHUNK, CHUNK), CHUNK)
+            dst[rows, :] = jnp.dot(weights[rows, :], block, preferred_element_type=jnp.float32)
+            return carry
+
+        lax.fori_loop(0, CENTS // CHUNK, part, 0)
 
     partial_in = []
     for b in range(2):
-        nsend[b] = product(other * 4 + 2 * b)
+        product(other * 4 + 2 * b, nsend.at[b])
         partial_in.append(remote(nsend.at[b], nrecv.at[b], fs.at[b], fr.at[b], sibling))
 
     mass_in.wait_recv()
@@ -302,13 +304,26 @@
         mass_ref[b:b + 1, :] = jnp.sum(
             jnp.where(diagonal, col_sum[LANES * b:LANES * (b + 1), :], 0.0), axis=0, keepdims=True)
 
+    outs = []
     for b in range(2):
         lanes = slice(256 * b, 256 * (b + 1))
-        own = product(core * 4 + 2 * b)
+        product(core * 4 + 2 * b, own.at[b])
         partial_in[b].wait_recv()
-        scale = 1.0 / (col_sum[...] + PRIOR)
-        out_ref[:, lanes] = (own + nrecv[b] + PRIOR * cent_ref[:, lanes]) * jnp.concatenate([scale, scale], axis=1)
-
+
+        def finish(m, carry):
+            rows = pl.ds(pl.multiple_of(m * 64, 64), 64)
+            scale = 1.0 / (col_sum[rows, :] + PRIOR)
+            total = own[b, rows, :] + nrecv[b, rows, :] + PRIOR * cent_ref[rows, lanes]
+            fresh[rows, lanes] = total * jnp.concatenate([scale, scale], axis=1)
+            return carry
+
+        lax.fori_loop(0, CENTS // 64, finish, 0)
+        out = pltpu.make_async_copy(fresh.at[:, lanes], out_ref.at[:, lanes], ls.at[2 + b])
+        out.start()
+        outs.append(out)
+
+    for out in outs:
+        out.wait()
     for copy in pending + partial_in + [mass_in]:
         copy.wait_send()
 
@@ -317,11 +332,11 @@
     vmem = pl.BlockSpec(memory_space=pltpu.VMEM)
     hbm = pl.BlockSpec(memory_space=pl.ANY)
     f32, bf16 = jnp.float32, jnp.bfloat16
-    fresh, mass = pl.pallas_call(
+    centers, mass = pl.pallas_call(
         kernel,
         out_shape=(jax.ShapeDtypeStruct((CENTS, HALF), f32), jax.ShapeDtypeStruct((8, LANES), f32)),
         in_specs=[hbm, hbm],
-        out_specs=(vmem, vmem),
+        out_specs=(hbm, vmem),
         scratch_shapes=[
             pltpu.VMEM((2 * ROWS, HALF), bf16),
             pltpu.VMEM((CENTS, HALF), f32),
@@ -342,18 +357,20 @@
             pltpu.VMEM((8, LANES), f32),
             pltpu.VMEM((2, CENTS, 256), f32),
             pltpu.VMEM((2, CENTS, 256), f32),
+            pltpu.VMEM((2, CENTS, 256), f32),
+            pltpu.VMEM((CENTS, HALF), f32),
             pltpu.SemaphoreType.DMA((GATHER_SEMS,)),
             pltpu.SemaphoreType.DMA((GATHER_SEMS,)),
             pltpu.SemaphoreType.DMA((ITERS, STAGE_SEMS)),
             pltpu.SemaphoreType.DMA((ITERS, STAGE_SEMS)),
             pltpu.SemaphoreType.DMA((3,)),
             pltpu.SemaphoreType.DMA((3,)),
-            pltpu.SemaphoreType.DMA((2,)),
+            pltpu.SemaphoreType.DMA((4,)),
         ],
         compiler_params=pltpu.CompilerParams(
             collective_id=0, has_side_effects=True, vmem_limit_bytes=60 * 1024 * 1024),
     )(points, centroids)
-    return fresh, mass.reshape(CENTS)
+    return centers, mass.reshape(CENTS)
 
 
 def solution(mesh):

time: 110 us -> 105 us (0.955)
  Pallas kernels: 105 us -> 100 us
    pallas_call x1, Pallas kernels: 105 us -> 100 us  [per_device(): pl.pallas_call(kernel, out_shape=(jax.ShapeDtypeStruct((CENTS, HALF), f32...]
where the time goes in v3:
time: 105 us
  Pallas kernels  100 us (95%)
  local copies, waits for them, and re-layouts  3.68 us (4%)
    pallas_call x1, Pallas kernels, per_device(): pl.pallas_call(kernel, out_shape=(jax.ShapeDtypeStruct((CENTS, HALF), f32...  100 us
    unnamed x4, local copies, waits for them, and re-layouts  3.68 us

profile of v3, /device:TPU:1, one launch (start us, length us, event | category | flops | bytes accessed | tf_op | source)
XLA Modules:
  0.0 104.6 jit_solution(8944716887381698969)
XLA Ops:
  0.6 100.3 %shard_map.41 = (f32[1024,512]{1,0:T(8,128)}, f32[8,128]{1,0:T(8,128)}) custom-call(bf16[32,512]{1,0:T(8,128)(2,1)} %points_hbm.1, f32[1024,512]{1,0:T(8,128)} %cent_hbm.1), custom_call_target="tpu_custom_call" | custom-call | tf_op jit(solution)/shard_map/pallas_call | solution.py:335
  100.9 0.0 copy-start
  101.0 3.1 %copy.6 = f32[1024,512]{1,0:T(8,128)} copy(f32[1024,512]{1,0:T(8,128)} %get-tuple-element.8) | data formatting | bytes 4194304
  104.0 0.0 copy-done
  104.0 0.6 copy.7
Async XLA Ops:
  100.9 3.1 %copy-start = (f32[8,128]{1,0:T(8,128)S(1)}, f32[8,128]{1,0:T(8,128)}, u32[]{:S(2)}) copy-start(f32[8,128]{1,0:T(8,128)} %get-tuple-element.5) | copy-start | bytes 12292

commit v4 on v3

--- a/solution.py
+++ b/solution.py
@@ -201,28 +201,40 @@
         top = reduce(jnp.maximum, parts)
         return top + jnp.log2(sum(jnp.exp2(p - top) for p in parts))
 
-    rpot[...] = jnp.zeros((PBLOCKS, LANES), jnp.float32)
-
-    def sweep(it, carry):
-        def col_block(g, c):
-            rows = pl.ds(pl.multiple_of(g * 16, 16), 16)
-            vals = [logits[rows, LANES * j:LANES * (j + 1)] + rpot[j:j + 1, :] for j in range(PBLOCKS)]
+    def col_pass(h):
+        def block(g, c):
+            rows = pl.ds(pl.multiple_of(g * 32, 32), 32)
+            vals = [logits[rows, LANES * j:LANES * (j + 1)] + rpot[j:j + 1, :] for j in range(8 * h, 8 * h + 8)]
             top = reduce(jnp.maximum, vals)
+            if h:
+                before = col_max[rows, :]
+                top = jnp.maximum(top, before)
+            total = sum(jnp.exp2(v - top) for v in vals)
+            if h:
+                total = total + col_sum[rows, :] * jnp.exp2(before - top)
             col_max[rows, :] = top
-            col_sum[rows, :] = sum(jnp.exp2(v - top) for v in vals)
+            col_sum[rows, :] = total
             return c
 
-        lax.fori_loop(0, CENTS // 16, col_block, 0, unroll=4)
-
-        top = jnp.max(col_max[...], axis=1, keepdims=True)
-        total = jnp.sum(col_sum[...] * jnp.exp2(col_max[...] - top), axis=1, keepdims=True)
-        mine = compact(top + jnp.log2(total))
-        csend[it] = mine
-        pair = remote(csend.at[it], crecv.at[it], its.at[it, STAGE_SEMS - 1], itr.at[it, STAGE_SEMS - 1], sibling)
-        pair.wait_recv()
-        spread(cpot, -LOG2_CENTS - merge([mine, crecv[it]]))
-
-        for jb in range(4):
+        lax.fori_loop(0, CENTS // 32, block, 0, unroll=4)
+
+    def plan_pass(h):
+        def block(g, c):
+            rows = pl.ds(pl.multiple_of(g * 32, 32), 32)
+            pot = cpot[rows, :] + LOG2_POINTS
+            total = col_sum[rows, :] if h else None
+            for j in range(8 * h, 8 * h + 8):
+                lanes = slice(LANES * j, LANES * (j + 1))
+                value = jnp.exp2(logits[rows, lanes] + rpot[j:j + 1, :] + pot)
+                weights[rows, lanes] = value.astype(jnp.bfloat16)
+                total = value if total is None else total + value
+            col_sum[rows, :] = total
+            return c
+
+        lax.fori_loop(0, CENTS // 32, block, 0, unroll=4)
+
+    def row_pass(it, h):
+        for jb in (2 * h, 2 * h + 1):
             def row_block(q, carry):
                 tops, sums = carry
                 rows = pl.ds(pl.multiple_of(q * 64, 64), 64)
@@ -242,40 +254,53 @@
             for j in range(4):
                 top = jnp.max(tops[j], axis=0, keepdims=True)
                 total = jnp.sum(sums[j] * jnp.exp2(tops[j] - top), axis=0, keepdims=True)
-                rsend[it, 0, 4 * jb + j:4 * jb + j + 1, :] = top + jnp.log2(total)
-
-        merged = None
-        sent = [pair]
-        for k, (base, n) in enumerate(STAGES):
-            peers = [at(0, dx, dy) for dx, dy in PLANE] if k == 0 else [at(d, 0, 0) for d in range(1, NZ)]
-            if k:
-                rsend[it, k] = merged
-            copies = [remote(rsend.at[it, k], rrecv.at[it, base + q], its.at[it, base + q], itr.at[it, base + q], peer)
-                      for q, peer in enumerate(peers)]
-            for copy in copies:
-                copy.wait_recv()
-            merged = merge([rsend[it, k]] + [rrecv[it, base + q] for q in range(n)])
-            sent += copies
-        rpot[...] = -LOG2_POINTS - merged
-        for copy in sent:
+                row = 4 * (jb % 2) + j
+                rsend[it, h, 0, row:row + 1, :] = top + jnp.log2(total)
+
+    def start(it, h, k):
+        base, _ = STAGES[k]
+        peers = [at(0, dx, dy) for dx, dy in PLANE] if k == 0 else [at(d, 0, 0) for d in range(1, NZ)]
+        return [remote(rsend.at[it, h, k], rrecv.at[it, h, base + q], its.at[it, h, base + q],
+                       itr.at[it, h, base + q], peer) for q, peer in enumerate(peers)]
+
+    def collect(it, h, k, copies):
+        base, n = STAGES[k]
+        for copy in copies:
+            copy.wait_recv()
+        return merge([rsend[it, h, k]] + [rrecv[it, h, base + q] for q in range(n)])
+
+    def sweep(it, tail):
+        top = jnp.max(col_max[...], axis=1, keepdims=True)
+        total = jnp.sum(col_sum[...] * jnp.exp2(col_max[...] - top), axis=1, keepdims=True)
+        mine = compact(top + jnp.log2(total))
+        csend[it] = mine
+        pair = remote(csend.at[it], crecv.at[it], its.at[it, 0, STAGE_SEMS - 1], itr.at[it, 0, STAGE_SEMS - 1],
+                      sibling)
+        pair.wait_recv()
+        spread(cpot, -LOG2_CENTS - merge([mine, crecv[it]]))
+        plane_out, z_out = [], []
+        for h in range(2):
+            row_pass(it, h)
+            plane_out.append(start(it, h, 0))
+        for h in range(2):
+            rsend[it, h, 1] = collect(it, h, 0, plane_out[h])
+            z_out.append(start(it, h, 1))
+        for h in range(2):
+            rpot[8 * h:8 * h + 8, :] = -LOG2_POINTS - collect(it, h, 1, z_out[h])
+            tail(h)
+        for copy in [pair] + plane_out[0] + plane_out[1] + z_out[0] + z_out[1]:
             copy.wait_send()
+
+    rpot[...] = jnp.zeros((PBLOCKS, LANES), jnp.float32)
+    col_pass(0)
+    col_pass(1)
+
+    def inner(it, carry):
+        sweep(it, col_pass)
         return carry
 
-    lax.fori_loop(0, ITERS, sweep, 0)
-
-    def plan_block(g, c):
-        rows = pl.ds(pl.multiple_of(g * 16, 16), 16)
-        pot = cpot[rows, :] + LOG2_POINTS
-        total = None
-        for j in range(PBLOCKS):
-            lanes = slice(LANES * j, LANES * (j + 1))
-            value = jnp.exp2(logits[rows, lanes] + rpot[j:j + 1, :] + pot)
-            weights[rows, lanes] = value.astype(jnp.bfloat16)
-            total = value if total is None else total + value
-        col_sum[rows, :] = total
-        return c
-
-    lax.fori_loop(0, CENTS // 16, plan_block, 0, unroll=4)
+    lax.fori_loop(0, ITERS - 1, inner, 0)
+    sweep(ITERS - 1, plan_pass)
 
     mine = compact(jnp.sum(col_sum[...], axis=1, keepdims=True))
     msend[...] = mine
@@ -351,8 +376,8 @@
             pltpu.VMEM((PBLOCKS, LANES), f32),
             pltpu.VMEM((ITERS, 8, LANES), f32),
             pltpu.VMEM((ITERS, 8, LANES), f32),
-            pltpu.VMEM((ITERS, len(STAGES), PBLOCKS, LANES), f32),
-            pltpu.VMEM((ITERS, STAGE_SEMS - 1, PBLOCKS, LANES), f32),
+            pltpu.VMEM((ITERS, 2, len(STAGES), 8, LANES), f32),
+            pltpu.VMEM((ITERS, 2, STAGE_SEMS - 1, 8, LANES), f32),
             pltpu.VMEM((8, LANES), f32),
             pltpu.VMEM((8, LANES), f32),
             pltpu.VMEM((2, CENTS, 256), f32),
@@ -361,8 +386,8 @@
             pltpu.VMEM((CENTS, HALF), f32),
             pltpu.SemaphoreType.DMA((GATHER_SEMS,)),
             pltpu.SemaphoreType.DMA((GATHER_SEMS,)),
-            pltpu.SemaphoreType.DMA((ITERS, STAGE_SEMS)),
-            pltpu.SemaphoreType.DMA((ITERS, STAGE_SEMS)),
+            pltpu.SemaphoreType.DMA((ITERS, 2, STAGE_SEMS)),
+            pltpu.SemaphoreType.DMA((ITERS, 2, STAGE_SEMS)),
             pltpu.SemaphoreType.DMA((3,)),
             pltpu.SemaphoreType.DMA((3,)),
             pltpu.SemaphoreType.DMA((4,)),

time: 105 us -> 101 us (0.962)
  Pallas kernels: 100 us -> 96.4 us
    pallas_call x1, Pallas kernels: 100 us -> 96.4 us  [per_device(): pl.pallas_call(kernel, out_shape=(jax.ShapeDtypeStruct((CENTS, HALF), f32...]
where the time goes in v4:
time: 101 us
  Pallas kernels  96.4 us (95%)
  local copies, waits for them, and re-layouts  3.68 us (4%)
    pallas_call x1, Pallas kernels, per_device(): pl.pallas_call(kernel, out_shape=(jax.ShapeDtypeStruct((CENTS, HALF), f32...  96.4 us
    unnamed x4, local copies, waits for them, and re-layouts  3.68 us

profile of v4, /device:TPU:1, one launch (start us, length us, event | category | flops | bytes accessed | tf_op | source)
XLA Modules:
  0.0 100.8 jit_solution(8861272645648498998)
XLA Ops:
  0.6 96.4 %shard_map.41 = (f32[1024,512]{1,0:T(8,128)}, f32[8,128]{1,0:T(8,128)}) custom-call(bf16[32,512]{1,0:T(8,128)(2,1)} %points_hbm.1, f32[1024,512]{1,0:T(8,128)} %cent_hbm.1), custom_call_target="tpu_custom_call" | custom-call | tf_op jit(solution)/shard_map/pallas_call | solution.py:360
  97.1 0.0 copy-start
  97.1 3.1 %copy.6 = f32[1024,512]{1,0:T(8,128)} copy(f32[1024,512]{1,0:T(8,128)} %get-tuple-element.8) | data formatting | bytes 4194304
  100.2 0.0 copy-done
  100.2 0.6 copy.7
Async XLA Ops:
  97.1 3.1 %copy-start = (f32[8,128]{1,0:T(8,128)S(1)}, f32[8,128]{1,0:T(8,128)}, u32[]{:S(2)}) copy-start(f32[8,128]{1,0:T(8,128)} %get-tuple-element.5) | copy-start | bytes 12292

commit v5 on v4

--- a/solution.py
+++ b/solution.py
@@ -23,6 +23,7 @@
 LOG2_CENTS = 17.0
 PRIOR = 4096 / 131072
 CHUNK = 256
+BLOCK = 512
 MESH = pl.DeviceIdType.MESH
 GATHER_SEMS = 148
 PLANE = tuple((dx, dy) for dx in range(NX) for dy in range(NY) if dx or dy)
@@ -30,7 +31,7 @@
 STAGE_SEMS = len(PLANE) + NZ
 
 
-def kernel(points_hbm, cent_hbm, out_ref, mass_ref, points_ref, cent_ref, pts, swap, cbf, logits, weights,
+def kernel(points_hbm, cent_hbm, out_ref, mass_ref, spread_ref, points_ref, cent_ref, pts, swap, cbf, logits, weights,
            col_max, col_sum, cpot, rpot, csend, crecv, rsend, rrecv, msend, mrecv, nsend, nrecv, own, fresh,
            gs, gr, its, itr, fs, fr, ls):
     blk = lax.axis_index("blk")
@@ -323,13 +324,15 @@
 
     mass_in.wait_recv()
     spread(col_sum, mine + mrecv[...])
+    masses_out = pltpu.make_async_copy(col_sum, spread_ref, ls.at[4])
+    masses_out.start()
     diagonal = (lax.broadcasted_iota(jnp.int32, (LANES, LANES), 0)
                 == lax.broadcasted_iota(jnp.int32, (LANES, LANES), 1))
     for b in range(8):
         mass_ref[b:b + 1, :] = jnp.sum(
             jnp.where(diagonal, col_sum[LANES * b:LANES * (b + 1), :], 0.0), axis=0, keepdims=True)
 
-    outs = []
+    outs = [masses_out]
     for b in range(2):
         lanes = slice(256 * b, 256 * (b + 1))
         product(core * 4 + 2 * b, own.at[b])
@@ -337,9 +340,7 @@
 
         def finish(m, carry):
             rows = pl.ds(pl.multiple_of(m * 64, 64), 64)
-            scale = 1.0 / (col_sum[rows, :] + PRIOR)
-            total = own[b, rows, :] + nrecv[b, rows, :] + PRIOR * cent_ref[rows, lanes]
-            fresh[rows, lanes] = total * jnp.concatenate([scale, scale], axis=1)
+            fresh[rows, lanes] = own[b, rows, :] + nrecv[b, rows, :] + PRIOR * cent_ref[rows, lanes]
             return carry
 
         lax.fori_loop(0, CENTS // 64, finish, 0)
@@ -353,15 +354,22 @@
         copy.wait_send()
 
 
+def divide(total_ref, spread_ref, mass_ref, out_ref, mass_out):
+    scale = 1.0 / (spread_ref[...] + PRIOR)
+    mass_out[...] = mass_ref[...]
+    out_ref[...] = total_ref[...] * jnp.concatenate([scale] * (HALF // LANES), axis=1)
+
+
 def per_device(points, centroids):
     vmem = pl.BlockSpec(memory_space=pltpu.VMEM)
     hbm = pl.BlockSpec(memory_space=pl.ANY)
     f32, bf16 = jnp.float32, jnp.bfloat16
-    centers, mass = pl.pallas_call(
+    total, mass, masses = pl.pallas_call(
         kernel,
-        out_shape=(jax.ShapeDtypeStruct((CENTS, HALF), f32), jax.ShapeDtypeStruct((8, LANES), f32)),
+        out_shape=(jax.ShapeDtypeStruct((CENTS, HALF), f32), jax.ShapeDtypeStruct((8, LANES), f32),
+                   jax.ShapeDtypeStruct((CENTS, LANES), f32)),
         in_specs=[hbm, hbm],
-        out_specs=(hbm, vmem),
+        out_specs=(hbm, vmem, hbm),
         scratch_shapes=[
             pltpu.VMEM((2 * ROWS, HALF), bf16),
             pltpu.VMEM((CENTS, HALF), f32),
@@ -390,11 +398,19 @@
             pltpu.SemaphoreType.DMA((ITERS, 2, STAGE_SEMS)),
             pltpu.SemaphoreType.DMA((3,)),
             pltpu.SemaphoreType.DMA((3,)),
-            pltpu.SemaphoreType.DMA((4,)),
+            pltpu.SemaphoreType.DMA((5,)),
         ],
         compiler_params=pltpu.CompilerParams(
             collective_id=0, has_side_effects=True, vmem_limit_bytes=60 * 1024 * 1024),
     )(points, centroids)
+    centers, mass = pl.pallas_call(
+        divide,
+        out_shape=(jax.ShapeDtypeStruct((CENTS, HALF), f32), jax.ShapeDtypeStruct((8, LANES), f32)),
+        grid=(CENTS // BLOCK,),
+        in_specs=[pl.BlockSpec((BLOCK, HALF), lambda i: (i, 0)), pl.BlockSpec((BLOCK, LANES), lambda i: (i, 0)),
+                  pl.BlockSpec((8, LANES), lambda i: (0, 0))],
+        out_specs=(pl.BlockSpec((BLOCK, HALF), lambda i: (i, 0)), pl.BlockSpec((8, LANES), lambda i: (0, 0))),
+    )(total, masses, mass)
     return centers, mass.reshape(CENTS)
 
 

time: 101 us -> 99.7 us (0.987)
  local copies, waits for them, and re-layouts: 3.68 us -> 0 us
  Pallas kernels: 96.4 us -> 98.9 us
    unnamed x4 -> x0, local copies, waits for them, and re-layouts: 3.68 us -> none
    pallas_call x0 -> x1, Pallas kernels: none -> 2.73 us  [per_device(): pl.pallas_call(divide, out_shape=(jax.ShapeDtypeStruct((CENTS, HALF), f32...]
where the time goes in v5:
time: 99.7 us; the launch traced here: 99.6 us
  Pallas kernels  98.9 us (99%)
    pallas_call x1, Pallas kernels, per_device(): pl.pallas_call(kernel, out_shape=(jax.ShapeDtypeStruct((CENTS, HALF), f32...  96.2 us
    pallas_call x1, Pallas kernels, per_device(): pl.pallas_call(divide, out_shape=(jax.ShapeDtypeStruct((CENTS, HALF), f32...  2.73 us

profile of v5, /device:TPU:1, one launch (start us, length us, event | category | flops | bytes accessed | tf_op | source)
XLA Modules:
  0.0 99.6 jit_solution(8303561977019669899)
XLA Ops:
  0.6 96.2 %shard_map.41 = (f32[1024,512]{1,0:T(8,128)}, f32[8,128]{1,0:T(8,128)}, f32[1024,128]{1,0:T(8,128)}) custom-call(bf16[32,512]{1,0:T(8,128)(2,1)} %points_hbm.1, f32[1024,512]{1,0:T(8,128)} %cent_hbm.1), custom_call_target="tpu_custom_call" | custom-call | tf_op jit(solution)/shard_map/pallas_call | solution.py:367
  96.8 2.7 %shard_map.42 = (f32[1024,512]{1,0:T(8,128)}, f32[8,128]{1,0:T(8,128)}) custom-call(f32[1024,512]{1,0:T(8,128)} %get-tuple-element.7.total_ref, f32[1024,128]{1,0:T(8,128)} %get-tuple-element.8.spread_ref, f32[8,128]{1,0:T(8,128)} %get-tuple-element.9.mass_ref), custom_call_target="tpu_custom_call" | custom-call | tf_op jit(solution)/shard_map/pallas_call | solution.py:406

commit v6 on v5

--- a/solution.py
+++ b/solution.py
@@ -22,11 +22,13 @@
 LOG2_POINTS = 12.0
 LOG2_CENTS = 17.0
 PRIOR = 4096 / 131072
-CHUNK = 256
+CHUNK = 512
 BLOCK = 512
 MESH = pl.DeviceIdType.MESH
 GATHER_SEMS = 148
-PLANE = tuple((dx, dy) for dx in range(NX) for dy in range(NY) if dx or dy)
+PLANE = tuple(sorted(((dx, dy) for dx in range(NX) for dy in range(NY) if dx or dy),
+                     key=lambda d: -min(d[0], NX - d[0]) - min(d[1], NY - d[1])))
+LAYERS = (4, 3, 5, 2, 6, 1, 7)
 STAGES = ((0, len(PLANE)), (len(PLANE), NZ - 1))
 STAGE_SEMS = len(PLANE) + NZ
 
@@ -260,7 +262,7 @@
 
     def start(it, h, k):
         base, _ = STAGES[k]
-        peers = [at(0, dx, dy) for dx, dy in PLANE] if k == 0 else [at(d, 0, 0) for d in range(1, NZ)]
+        peers = [at(0, dx, dy) for dx, dy in PLANE] if k == 0 else [at(d, 0, 0) for d in LAYERS]
         return [remote(rsend.at[it, h, k], rrecv.at[it, h, base + q], its.at[it, h, base + q],
                        itr.at[it, h, base + q], peer) for q, peer in enumerate(peers)]
 

time: 99.7 us -> 95.6 us (0.959)
  Pallas kernels: 98.9 us -> 94.8 us
    pallas_call x1, Pallas kernels: 96.2 us -> 92.1 us  [per_device(): pl.pallas_call(kernel, out_shape=(jax.ShapeDtypeStruct((CENTS, HALF), f32...]
where the time goes in v6:
time: 95.6 us; the launch traced here: 95.4 us
  Pallas kernels  94.8 us (99%)
    pallas_call x1, Pallas kernels, per_device(): pl.pallas_call(kernel, out_shape=(jax.ShapeDtypeStruct((CENTS, HALF), f32...  92.1 us
    pallas_call x1, Pallas kernels, per_device(): pl.pallas_call(divide, out_shape=(jax.ShapeDtypeStruct((CENTS, HALF), f32...  2.73 us

profile of v6, /device:TPU:1, one launch (start us, length us, event | category | flops | bytes accessed | tf_op | source)
XLA Modules:
  0.0 95.4 jit_solution(432006268083234220)
XLA Ops:
  0.6 92.1 %shard_map.41 = (f32[1024,512]{1,0:T(8,128)}, f32[8,128]{1,0:T(8,128)}, f32[1024,128]{1,0:T(8,128)}) custom-call(bf16[32,512]{1,0:T(8,128)(2,1)} %points_hbm.1, f32[1024,512]{1,0:T(8,128)} %cent_hbm.1), custom_call_target="tpu_custom_call" | custom-call | tf_op jit(solution)/shard_map/pallas_call | solution.py:369
  92.7 2.7 %shard_map.42 = (f32[1024,512]{1,0:T(8,128)}, f32[8,128]{1,0:T(8,128)}) custom-call(f32[1024,512]{1,0:T(8,128)} %get-tuple-element.7.total_ref, f32[1024,128]{1,0:T(8,128)} %get-tuple-element.8.spread_ref, f32[8,128]{1,0:T(8,128)} %get-tuple-element.9.mass_ref), custom_call_target="tpu_custom_call" | custom-call | tf_op jit(solution)/shard_map/pallas_call | solution.py:408
